TPU v7x, 128 devices: a whole 4x4x4 slice. The times are simulated.
128 devices in a mesh: grp: 4 (over y), shard: 32 (over x, z, core).
Axes of the slice: x: 4, y: 4, z: 4, core: 2. Of those that a mesh axis runs over, the one named last changes fastest.
Arguments:
- new_rows: bfloat16 [32768, 1024], P(('grp', 'shard'))
- cluster_ids: int32 [32768], P(('grp', 'shard')), may hold values from 0 to 7, as said below
- new_order: int32 [32768], P(('grp', 'shard')), may hold values from 0 to 2147483646
- codes: bfloat16 [8, 8192, 1024], P('grp', 'shard'), may hold values from -8 to 8
- scales: float32 [8, 1024], P('grp')
- offsets: float32 [8, 1024], P('grp')
- counts: int32 [8], P('grp'), may hold values from 1024 to 8192, as said below
- earlier_order: int32 [8, 8192], P('grp', 'shard'), may hold values from 1 to 2147483646
Outputs:
- max_similarity: float32 [32768], P(('grp', 'shard'))
Inputs may be any that keep to these rules, and one draw needn't show every extreme that they name: `cluster_ids`: in each device's block of 256 rows, no group's clusters are named by more than 128 rows, and some group's clusters are named by exactly 128 rows. `counts`: some cluster has all 8192 slots live.
All inputs are finite; a program needn't handle non-finite values.
Results may differ from a plain program's by a relative error of at most 0.00047.
Values may be sent and summed in bfloat16 or wider, within the bound.
A program may use at most 128 MiB of HBM per device.

v0:
```python
import jax
import jax.numpy as jnp
from jax import lax
from jax.sharding import PartitionSpec as P

epsilon = 1e-06


def unit_rows(values):
    return (values / jnp.sqrt(jnp.sum(values * values, axis=-1, keepdims=True) + epsilon)).astype(
        jnp.bfloat16
    )


def score_clusters(
    running, queries, query_cluster, query_order, key_source, key_order, live_counts, prepare
):
    width = key_source.shape[1]
    positions = jnp.arange(width, dtype=jnp.int32)
    best = running
    for cluster in range(key_source.shape[0]):
        cluster_keys = prepare(key_source[cluster], cluster)
        scores = jnp.dot(queries, cluster_keys.T, preferred_element_type=jnp.float32)
        allowed = (
            (query_cluster[:, None] == cluster)
            & (positions[None, :] < live_counts[cluster])
            & (key_order[cluster][None, :] < query_order[:, None])
        )
        best = jnp.maximum(best, jnp.max(jnp.where(allowed, scores, -1.0), axis=1))
    return best


def per_device(new_rows, cluster_ids, new_order, codes, scales, offsets, counts, earlier_order):
    groups = lax.axis_size("grp")
    owned_count = codes.shape[0]
    local_rows = new_rows.shape[0]
    capacity = local_rows // 2
    queries = unit_rows(new_rows.astype(jnp.float32))
    target = cluster_ids // owned_count
    onehot = (target[:, None] == jnp.arange(groups, dtype=jnp.int32)[None, :]).astype(jnp.int32)
    slot_rank = jnp.sum((jnp.cumsum(onehot, axis=0) - onehot) * onehot, axis=1)
    position = target * capacity + slot_rank
    received = groups * capacity
    matches = position[None, :] == jnp.arange(received, dtype=jnp.int32)[:, None]
    filled = jnp.any(matches, axis=1)
    source_row = jnp.sum(
        jnp.where(matches, jnp.arange(local_rows, dtype=jnp.int32)[None, :], 0), axis=1
    )
    send_rows = jnp.take(queries, source_row, axis=0).reshape(groups, capacity, queries.shape[1])
    send_cluster = jnp.where(filled, jnp.take(cluster_ids % owned_count, source_row), 0).reshape(
        groups, capacity
    )
    send_order = jnp.where(filled, jnp.take(new_order, source_row), 0).reshape(groups, capacity)
    got_rows, got_cluster, got_order = (
        lax.all_to_all(send_rows, "grp", split_axis=0, concat_axis=0, tiled=True),
        lax.all_to_all(send_cluster, "grp", split_axis=0, concat_axis=0, tiled=True),
        lax.all_to_all(send_order, "grp", split_axis=0, concat_axis=0, tiled=True),
    )
    got_rows = got_rows.reshape(received, queries.shape[1])
    got_cluster = got_cluster.reshape(received)
    got_order = got_order.reshape(received)
    starting = jnp.zeros((received,), jnp.float32)

    def decode_one(code_rows, cluster):
        return unit_rows(
            code_rows.astype(jnp.float32) * scales[cluster][None, :] + offsets[cluster][None, :]
        )

    top_score = score_clusters(
        starting,
        got_rows,
        got_cluster,
        got_order,
        lax.all_gather(codes, "shard", axis=1, tiled=True),
        lax.all_gather(earlier_order, "shard", axis=1, tiled=True),
        counts,
        decode_one,
    )
    answered = lax.all_to_all(
        top_score.reshape(groups, capacity), "grp", split_axis=0, concat_axis=0, tiled=True
    )
    return jnp.take(answered.reshape(received), position)


def solution(mesh):
    return jax.shard_map(
        per_device,
        mesh=mesh,
        in_specs=(
            P(("grp", "shard"), None),
            P(("grp", "shard")),
            P(("grp", "shard")),
            P("grp", "shard", None),
            P("grp", None),
            P("grp", None),
            P("grp"),
            P("grp", "shard"),
        ),
        out_specs=P(("grp", "shard")),
        check_vma=False,
    )
```

profile of v0, /device:TPU:0, one launch (start us, length us, event | category | flops | bytes accessed | tf_op | source)
XLA Modules:
  0.0 194.7 jit_solution(17353483784496994221)
XLA Ops:
  6.5 0.0 copy-start
  6.5 0.0 all-gather.2.cloned.1.call-start
  6.5 0.7 all-gather.2.cloned.1.call-update
  7.3 0.7 and_select_fusion
  8.0 1.2 reduce-window.6
  9.2 0.1 slice.56
  9.3 0.1 copy.15
  9.4 0.1 copy.16
  9.5 0.1 add_bitcast_fusion
  9.6 0.6 compare_select_fusion.3
  10.2 0.0 copy-start.1
  10.2 0.1 select_reduce_fusion.2
  10.3 3.5 %gather_fusion.2 = s32[512]{0:T(512)S(1)} fusion(s32[256]{0:T(256)S(1)} %get-tuple-element.20, s32[1024]{0:T(1024)S(1)} %pad_clamp_fusion.2), kind=kCustom, calls=%fused_computation.clone | custom fusion | bytes 6144 | tf_op jit(solution)/shard_map/jit(_take)/gather | solution.py:50
  13.9 0.0 copy-done
  13.9 3.5 %gather_fusion.3 = s32[512]{0:T(512)S(1)} fusion(s32[256]{0:T(256)S(1)} %copy-done, s32[1024]{0:T(1024)S(1)} %pad_clamp_fusion.2), kind=kCustom, calls=%fused_computation.1.clone | custom fusion | bytes 6144 | tf_op jit(solution)/shard_map/jit(_take)/gather | solution.py:53
  17.4 0.2 fusion.28
  17.6 0.5 select_select_fusion.1
  18.1 4.5 %all-to-all-start = ((s32[4,1,128]{2,1,0:T(1,128)}), s32[4,1,128]{2,1,0:T(1,128)S(1)}, u32[]{:S(2)}, u32[]{:S(2)}) async-start(s32[4,1,128]{2,1,0:T(1,128)} %bitcast.3), calls=%async_computation | async-start | bytes 4096 | tf_op jit(solution)/shard_map/all_to_all | solution.py:56
  22.7 1.3 fusion.26
  24.0 0.0 copy-done.1
  24.0 1.4 fusion.27
  25.3 2.1 %gather_fusion = bf16[512,1024]{1,0:T(8,128)(2,1)S(1)} fusion(bf16[256,1024]{1,0:T(8,128)(2,1)S(1)} %fusion.27, s32[1024]{0:T(1024)S(1)} %pad_clamp_fusion.1), kind=kCustom, calls=%fused_computation.2 | custom fusion | bytes 2099200 | tf_op jit(solution)/shard_map/jit(_take)/gather | solution.py:49
  27.4 25.5 %all_gather.6 = s32[2,8192]{1,0:T(2,128)S(1)} all-gather(s32[2,256]{1,0:T(2,128)} %param.17), channel_id=1, replica_groups=mesh['grp'=4,'shard'=32] {'shard'}, dimensions={1}, use_global_device_ids=true | all-gather | bytes 67584 | tf_op jit(solution)/shard_map/all_gather | solution.py:75
  52.9 1.3 fusion.35
  54.2 0.7 iota_compare_fusion.2
  54.9 0.8 fusion.33
  55.7 0.8 fusion.34
  56.5 1.2 broadcast_select_fusion
  57.6 0.1 fusion.32
  57.7 0.6 iota_compare_fusion.1
  58.2 0.0 all-to-all-done
  58.2 4.7 %all-to-all-start.1 = ((s32[4,1,128]{2,1,0:T(1,128)}), s32[4,1,128]{2,1,0:T(1,128)S(1)}, u32[]{:S(2)}, u32[]{:S(2)}) async-start(s32[4,1,128]{2,1,0:T(1,128)} %bitcast.6), calls=%async_computation.1 | async-start | bytes 4096 | tf_op jit(solution)/shard_map/all_to_all | solution.py:57
  63.0 5.2 %all-to-all-done.1 = s32[4,1,128]{2,1,0:T(1,128)S(1)} async-done(((s32[4,1,128]{2,1,0:T(1,128)}), s32[4,1,128]{2,1,0:T(1,128)S(1)}, u32[]{:S(2)}, u32[]{:S(2)}) %all-to-all-start.1) | async-done | bytes 2080 | tf_op jit(solution)/shard_map/all_to_all | solution.py:57
  68.2 3.5 %all-to-all-start.2 = ((bf16[4,128,1024]{2,1,0:T(8,128)(2,1)}), bf16[4,128,1024]{2,1,0:T(8,128)(2,1)S(1)}, u32[]{:S(2)}, u32[]{:S(2)}) async-start(bf16[4,128,1024]{2,1,0:T(8,128)(2,1)} %broadcast_select_fusion), calls=%async_computation.2 | async-start | bytes 2097152 | tf_op jit(solution)/shard_map/all_to_all | solution.py:55
  71.8 54.4 %all-gather.2.cloned.1.call-done = bf16[2,8192,1024]{2,1,0:T(8,128)(2,1)} async-done(((bf16[2,256,1024]{2,1,0:T(8,128)(2,1)}), bf16[2,8192,1024]{2,1,0:T(8,128)(2,1)}) %all-gather.2.cloned.1.call-update) | async-done | bytes 33554448 | tf_op jit(solution)/shard_map/all_gather | solution.py:74
  126.2 20.2 %fusion.6 = (f32[8192]{0:T(1024)S(1)}, f32[8192]{0:T(1024)S(1)}) fusion(f32[1024]{0:T(1024)S(1)} %bitcast.89, f32[1024]{0:T(1024)S(1)} %bitcast.87, bf16[2,8192,1024]{2,1,0:T(8,128)(2,1)} %all-gather.2.cloned.1.call-done, f32[1024]{0:T(1024)S(1)} %bitcast.85, f32[1024]{0:T(1024)S(1)} %bitcast.83), kind=kLoop, calls=%fused_computation.14 | loop fusion | flops 83869696 | bytes 33636352 | tf_op jit(solution)/shard_map/reduce_sum | solution.py:10
  146.4 0.0 all-to-all-done.2
  146.4 14.4 %select_reduce_fusion.1 = f32[512]{0:T(512)S(1)} fusion(s32[8192]{0:T(1024)S(1)} %bitcast.81, s32[512]{0:T(512)S(1)} %bitcast.93, pred[8192]{0:T(1024)(128)(4,1)S(1)} %iota_compare_fusion.2, pred[512]{0:T(512)(128)(4,1)S(1)} %bitcast.96, bf16[512,1024]{1,0:T(8,128)(2,1)S(1)} %bitcast.77, f32[8192]{0:T(1024)S(1)} %get-tuple-element.25, ...), kind=kOutput, calls=%fused_computation.25 | convolution fusion | flops 8652849152 | bytes 17912320 | tf_op jit(solution)/shard_map/dot_general | solution.py:23
  160.8 0.0 copy-start.3
  160.8 0.0 copy-start.2
  160.9 14.5 %select_reduce_fusion = f32[512]{0:T(512)S(1)} fusion(s32[8192]{0:T(1024)S(1)} %bitcast.80, s32[512]{0:T(512)S(1)} %bitcast.94, pred[8192]{0:T(1024)(128)(4,1)S(1)} %iota_compare_fusion.1, pred[512]{0:T(512)(128)(4,1)S(1)} %bitcast.95, bf16[512,1024]{1,0:T(8,128)(2,1)S(1)} %bitcast.78, f32[8192]{0:T(1024)S(1)} %get-tuple-element.24, f32[1024]{0:T(1024)S(1)} %bitcast.86, ...), kind=kOutput, calls=%fused_computation.24 | convolution fusion | flops 8652849152 | bytes 17912320 | tf_op jit(solution)/shard_map/dot_general | solution.py:23
  175.3 0.6 maximum_maximum_fusion
  175.9 4.3 %all-to-all-start.3 = ((f32[4,1,128]{2,1,0:T(1,128)}), f32[4,1,128]{2,1,0:T(1,128)S(1)}, u32[]{:S(2)}, u32[]{:S(2)}) async-start(f32[4,1,128]{2,1,0:T(1,128)} %bitcast.23), calls=%async_computation.3 | async-start | bytes 4096 | tf_op jit(solution)/shard_map/all_to_all | solution.py:79
  180.2 0.0 copy-done.3
  180.2 5.1 %all-to-all-done.3 = f32[4,1,128]{2,1,0:T(1,128)S(1)} async-done(((f32[4,1,128]{2,1,0:T(1,128)}), f32[4,1,128]{2,1,0:T(1,128)S(1)}, u32[]{:S(2)}, u32[]{:S(2)}) %all-to-all-start.3) | async-done | bytes 2080 | tf_op jit(solution)/shard_map/all_to_all | solution.py:79
  185.3 1.9 gather_fusion.1
  187.3 0.0 copy-done.2
  187.3 0.6 and_select_fusion.1
  (13 shorter events, 0.2 us)
Async XLA Ops:
  6.5 7.3 %copy-start = (s32[256]{0:T(256)S(1)}, s32[256]{0:T(256)}, u32[]{:S(2)}) copy-start(s32[256]{0:T(256)} %param.12) | copy-start | bytes 3076
  6.5 119.7 %all-gather.2.cloned.1.call-start = ((), (), s32[]{:S(2)}) async-start(), calls=%async_computation.4 | async-start | bytes 34603008 | tf_op jit(solution)/shard_map/all_gather | solution.py:74
  10.2 13.8 %copy-start.1 = (s32[256]{0:T(256)}, s32[256]{0:T(256)S(1)}, u32[]{:S(2)}) copy-start(s32[256]{0:T(256)S(1)} %get-tuple-element.11) | copy-start | bytes 3076
  18.1 40.1 %all-to-all-start = ((s32[4,1,128]{2,1,0:T(1,128)}), s32[4,1,128]{2,1,0:T(1,128)S(1)}, u32[]{:S(2)}, u32[]{:S(2)}) async-start(s32[4,1,128]{2,1,0:T(1,128)} %bitcast.3), calls=%async_computation | async-start | bytes 4096 | tf_op jit(solution)/shard_map/all_to_all | solution.py:56
  58.2 10.0 %all-to-all-start.1 = ((s32[4,1,128]{2,1,0:T(1,128)}), s32[4,1,128]{2,1,0:T(1,128)S(1)}, u32[]{:S(2)}, u32[]{:S(2)}) async-start(s32[4,1,128]{2,1,0:T(1,128)} %bitcast.6), calls=%async_computation.1 | async-start | bytes 4096 | tf_op jit(solution)/shard_map/all_to_all | solution.py:57
  68.2 78.2 %all-to-all-start.2 = ((bf16[4,128,1024]{2,1,0:T(8,128)(2,1)}), bf16[4,128,1024]{2,1,0:T(8,128)(2,1)S(1)}, u32[]{:S(2)}, u32[]{:S(2)}) async-start(bf16[4,128,1024]{2,1,0:T(8,128)(2,1)} %broadcast_select_fusion), calls=%async_computation.2 | async-start | bytes 2097152 | tf_op jit(solution)/shard_map/all_to_all | solution.py:55
  160.8 19.4 %copy-start.3 = (s32[256]{0:T(256)S(1)}, s32[256]{0:T(256)}, u32[]{:S(2)}) copy-start(s32[256]{0:T(256)} %get-tuple-element.10) | copy-start | bytes 3076
  160.8 26.4 %copy-start.2 = (s32[256]{0:T(256)S(1)}, s32[256]{0:T(256)}, u32[]{:S(2)}) copy-start(s32[256]{0:T(256)} %copy-done.1) | copy-start | bytes 3076
  175.9 9.4 %all-to-all-start.3 = ((f32[4,1,128]{2,1,0:T(1,128)}), f32[4,1,128]{2,1,0:T(1,128)S(1)}, u32[]{:S(2)}, u32[]{:S(2)}) async-start(f32[4,1,128]{2,1,0:T(1,128)} %bitcast.23), calls=%async_computation.3 | async-start | bytes 4096 | tf_op jit(solution)/shard_map/all_to_all | solution.py:79
Sparse Core Ops, SparseCore 0:
  9.7 116.4 all-gather.1
where the time goes:
time: 195 us
  waiting for transfers between devices  65.5 us (34%)
  other arithmetic  29.9 us (15%)
  matrix products  28.9 us (15%)
  blocking collectives  25.5 us (13%)
  starting transfers between devices  17.1 us (9%)
  local copies, waits for them, and re-layouts  14.3 us (7%)
  between operations  13.6 us (7%)
    all_gather x1, waiting for transfers between devices, per_device(): lax.all_gather(codes, 'shard', axis=1, tiled=True)  54.4 us
    dot_general x2, matrix products, score_clusters(): jnp.dot(queries, cluster_keys.T, preferred_element_type=jnp.float32)  28.9 us
    all_gather x1, blocking collectives, per_device(): lax.all_gather(earlier_order, 'shard', axis=1, tiled=True)  25.5 us
    reduce_sum x2, other arithmetic, unit_rows(): jnp.sum(values * values, axis=-1, keepdims=True) + epsilon  21.4 us
    all_to_all x1, waiting for transfers between devices, per_device(): lax.all_to_all(send_order, 'grp', split_axis=0, concat_axis=0, tiled=True)  5.23 us
    all_to_all x1, waiting for transfers between devices, per_device(): lax.all_to_all(top_score.reshape(groups, capacity), 'grp', split_axis=0,...  5.09 us
    all_to_all x1, starting transfers between devices, per_device(): lax.all_to_all(send_order, 'grp', split_axis=0, concat_axis=0, tiled=True)  4.72 us
    all_to_all x1, starting transfers between devices, per_device(): lax.all_to_all(send_cluster, 'grp', split_axis=0, concat_axis=0, tiled=True)  4.55 us
  transfers between devices with their start and end apart: 5, of which 3 were waited for; matrix products, arithmetic and copies ran while one was open for 21% of the time, Pallas kernels for 0%

commit v1 on v0

--- a/solution.py
+++ b/solution.py
@@ -4,6 +4,28 @@
 from jax.sharding import PartitionSpec as P
 
 epsilon = 1e-06
+
+
+def in_order(tiles, dim):
+    tiles = jnp.moveaxis(tiles, 0, dim)
+    shape = tiles.shape
+    return tiles.reshape(*shape[:dim], shape[dim] * shape[dim + 1], *shape[dim + 2 :])
+
+
+def doubled(array, axis):
+    size = lax.axis_size(axis)
+    blocks = array[None]
+    for level in range(size.bit_length() - 1):
+        distance = 1 << level
+        other = lax.ppermute(blocks, axis, [(i, i ^ distance) for i in range(size)])
+        both = jnp.stack([blocks, other])
+        upper = lax.axis_index(axis) >> level & 1
+        blocks = jnp.where(upper == 0, both, both[::-1]).reshape(-1, *array.shape)
+    return blocks
+
+
+def collect(x, axis, dim):
+    return in_order(doubled(x, axis), dim)
 
 
 def unit_rows(values):
@@ -71,7 +93,7 @@
         got_rows,
         got_cluster,
         got_order,
-        lax.all_gather(codes, "shard", axis=1, tiled=True),
+        collect(codes, "shard", 1),
         lax.all_gather(earlier_order, "shard", axis=1, tiled=True),
         counts,
         decode_one,

time: 195 us -> 913 us (4.68)
  blocking collectives: 25.5 us -> 360 us
  waiting for transfers between devices: 65.5 us -> 324 us
  other arithmetic: 29.9 us -> 159 us
  between operations: 13.6 us -> 0.3 us
  starting transfers between devices: 17.1 us -> 28.8 us
    all_gather x1, blocking collectives: 25.5 us -> 360 us  [per_device(): lax.all_gather(earlier_order, 'shard', axis=1, tiled=True)]
    ppermute x0 -> x5, waiting for transfers between devices: none -> 319 us  [doubled(): other = lax.ppermute(blocks, axis, [(i, i ^ distance) for i in range(size)])]
    select_n x0 -> x4, other arithmetic: none -> 60.6 us  [doubled(): blocks = jnp.where(upper == 0, both, both[::-1]).reshape(-1, *array.shape)]
    all_gather x1 -> x0, waiting for transfers between devices: 54.4 us -> none  [per_device(): lax.all_gather(codes, 'shard', axis=1, tiled=True)]
    another operation x2 -> x8, other arithmetic: 1.26 us -> 44.9 us  [the longest x6 43.7 us: doubled(): both = jnp.stack([blocks, other])]
    convert_element_type x1 -> x2, other arithmetic: 1.36 us -> 28.6 us  [unit_rows(): (values / jnp.sqrt(jnp.sum(values * values, axis=-1, keepdims=True) + eps...]
    ppermute x0 -> x5, starting transfers between devices: none -> 10.2 us  [doubled(): other = lax.ppermute(blocks, axis, [(i, i ^ distance) for i in range(size)])]
  transfers between devices with their start and end apart: 5 -> 9, of which waited for: 3 -> 5; matrix products, arithmetic and copies ran while one was open for 21% -> 13% of each run, Pallas kernels for 0% -> 0%
where the time goes in v1:
time: 913 us; the launch traced here: 912 us
  blocking collectives  360 us (39%)
  waiting for transfers between devices  324 us (35%)
  other arithmetic  159 us (17%)
  starting transfers between devices  28.8 us (3%)
  matrix products  27.3 us (3%)
  local copies, waits for them, and re-layouts  12 us (1%)
    all_gather x1, blocking collectives, per_device(): lax.all_gather(earlier_order, 'shard', axis=1, tiled=True)  360 us
    ppermute x5, waiting for transfers between devices, doubled(): other = lax.ppermute(blocks, axis, [(i, i ^ distance) for i in range(size)])  319 us
    select_n x4, other arithmetic, doubled(): blocks = jnp.where(upper == 0, both, both[::-1]).reshape(-1, *array.shape)  60.6 us
    another operation x6, other arithmetic, doubled(): both = jnp.stack([blocks, other])  43.7 us
    convert_element_type x2, other arithmetic, unit_rows(): (values / jnp.sqrt(jnp.sum(values * values, axis=-1, keepdims=True) + eps...  28.6 us
    dot_general x2, matrix products, score_clusters(): jnp.dot(queries, cluster_keys.T, preferred_element_type=jnp.float32)  27.3 us
    reduce_sum x2, other arithmetic, unit_rows(): jnp.sum(values * values, axis=-1, keepdims=True) + epsilon  20.5 us
  transfers between devices with their start and end apart: 9, of which 5 were waited for; matrix products, arithmetic and copies ran while one was open for 13% of the time, Pallas kernels for 0%

profile of v1, /device:TPU:0, one launch (start us, length us, event | category | flops | bytes accessed | tf_op | source)
XLA Modules:
  0.0 912.1 jit_solution(12397598160608921297)
XLA Ops:
  0.0 0.0 collective-permute-start
  0.0 2.9 collective-permute-done
  2.9 1.4 pad_maximum_fusion.4
  4.3 2.2 fusion.1
  6.5 2.0 collective-permute-start.1
  8.5 46.2 %collective-permute-done.1 = bf16[2,2,256,1024]{3,2,1,0:T(8,128)(2,1)} collective-permute-done((bf16[2,2,256,1024]{3,2,1,0:T(8,128)(2,1)}, bf16[2,2,256,1024]{3,2,1,0:T(8,128)(2,1)}, u32[]{:S(2)}, u32[]{:S(2)}) %collective-permute-start.1) | collective-permute-done | bytes 2097184 | tf_op jit(solution)/shard_map/ppermute | solution.py:20
  54.7 2.0 pad_maximum_fusion.3
  56.7 3.2 reverse_select_fusion.3
  59.9 3.7 collective-permute-start.2
  63.6 90.4 %collective-permute-done.2 = bf16[4,2,256,1024]{3,2,1,0:T(8,128)(2,1)} collective-permute-done((bf16[4,2,256,1024]{3,2,1,0:T(8,128)(2,1)}, bf16[4,2,256,1024]{3,2,1,0:T(8,128)(2,1)}, u32[]{:S(2)}, u32[]{:S(2)}) %collective-permute-start.2) | collective-permute-done | bytes 4194336 | tf_op jit(solution)/shard_map/ppermute | solution.py:20
  154.0 7.5 pad_maximum_fusion.2
  161.5 13.6 %reverse_select_fusion.2 = bf16[2,4,2,256,1024]{4,3,2,1,0:T(8,128)(2,1)} fusion(bf16[2,4,2,256,1024]{4,3,2,1,0:T(8,128)(2,1)} %pad_maximum_fusion.2, pred[]{:T(512)S(6)} %eq.96), kind=kLoop, calls=%fused_computation.16 | loop fusion | flops 4194304 | bytes 16777216 | tf_op jit(solution)/shard_map/jit(_where)/select_n | solution.py:23
  175.0 1.5 collective-permute-start.3
  176.5 179.9 %collective-permute-done.3 = bf16[8,2,256,1024]{3,2,1,0:T(8,128)(2,1)} collective-permute-done((bf16[8,2,256,1024]{3,2,1,0:T(8,128)(2,1)}, bf16[8,2,256,1024]{3,2,1,0:T(8,128)(2,1)}, u32[]{:S(2)}, u32[]{:S(2)}) %collective-permute-start.3) | collective-permute-done | bytes 8388640 | tf_op jit(solution)/shard_map/ppermute | solution.py:20
  356.4 8.0 pad_maximum_fusion.1
  364.4 0.0 copy-start.7
  364.4 0.0 copy-start.2
  364.4 0.0 copy-start.5
  364.4 0.0 copy-start.6
  364.5 0.0 copy-start.3
  364.5 0.0 copy-start.4
  364.5 10.5 %reverse_select_fusion.1 = bf16[2,8,2,256,1024]{4,3,2,1,0:T(8,128)(2,1)} fusion(bf16[2,8,2,256,1024]{4,3,2,1,0:T(8,128)(2,1)S(1)} %pad_maximum_fusion.1, pred[]{:T(512)S(6)} %eq.95), kind=kLoop, calls=%fused_computation.12 | loop fusion | flops 8388608 | bytes 33554432 | tf_op jit(solution)/shard_map/jit(_where)/select_n | solution.py:23
  375.0 3.0 collective-permute-start.4
  378.0 1.2 reduce-window.6
  379.3 0.1 slice.58
  379.3 0.1 copy.15
  379.5 0.1 copy.16
  379.6 0.1 add_bitcast_fusion
  379.7 0.2 select_reduce_fusion.2
  379.9 3.5 gather_fusion.2
  383.4 0.0 copy-done
  383.4 3.5 gather_fusion.3
  386.9 0.2 fusion.4
  387.1 0.6 select_select_fusion.1
  387.7 4.5 all-to-all-start
  392.2 0.2 fusion.2
  392.4 0.2 fusion.3
  392.6 2.1 gather_fusion
  394.7 0.0 copy-done.5
  394.7 359.8 %all_gather.3 = s32[2,8192]{1,0:T(2,128)S(1)} all-gather(s32[2,256]{1,0:T(2,128)S(1)} %copy-done.5), channel_id=1, replica_groups=mesh['grp'=4,'shard'=32] {'shard'}, dimensions={1}, use_global_device_ids=true | all-gather | bytes 67584 | tf_op jit(solution)/shard_map/all_gather | solution.py:97
  754.5 0.6 fusion.11
  755.1 0.7 iota_compare_fusion.2
  755.8 0.0 copy-done.4
  755.9 1.1 broadcast_select_fusion
  757.0 0.1 fusion.8
  757.1 0.6 iota_compare_fusion.1
  757.7 0.0 all-to-all-done
  757.7 4.5 all-to-all-start.1
  762.2 0.0 collective-permute-done.4
  762.2 22.6 %pad_maximum_fusion = bf16[2,16,2,256,1024]{4,3,2,1,0:T(8,128)(2,1)} fusion(bf16[1,16,2,256,1024]{4,3,2,1,0:T(8,128)(2,1)} %bitcast.27, bf16[1,16,2,256,1024]{4,3,2,1,0:T(8,128)(2,1)} %bitcast.25), kind=kLoop, calls=%fused_computation.5 | loop fusion | flops 16777216 | bytes 67108864 | tf_op jit(solution)/shard_map/stack | solution.py:21
  784.8 33.3 %reverse_select_fusion = bf16[2,16,2,256,1024]{4,3,2,1,0:T(8,128)(2,1)} fusion(bf16[2,16,2,256,1024]{4,3,2,1,0:T(8,128)(2,1)} %pad_maximum_fusion, pred[]{:T(512)S(6)} %eq.94), kind=kLoop, calls=%fused_computation.4 | loop fusion | flops 16777216 | bytes 67108864 | tf_op jit(solution)/shard_map/jit(_where)/select_n | solution.py:23
  818.2 20.3 %multiply_reduce_fusion.1 = (f32[32,256]{1,0:T(8,128)S(1)}, f32[32,256]{1,0:T(8,128)S(1)}) fusion(f32[1024]{0:T(1024)S(1)} %bitcast.89, f32[1024]{0:T(1024)S(1)} %bitcast.85, bf16[2,32,256,1024]{3,2,0,1:T(8,128)(2,1)} %bitcast.70, f32[1024]{0:T(1024)S(1)} %bitcast.87, f32[1024]{0:T(1024)S(1)} %bitcast.83), kind=kLoop, calls=%fused_computation.10 | loop fusion | flops 83869696 | bytes 33636352 | tf_op jit(solution)/shard_map/reduce_sum | solution.py:32
  838.5 0.0 all-to-all-done.1
  838.5 4.8 all-to-all-start.2
  843.3 28.4 %divide_convert_fusion.1 = (bf16[1,32,256,1024]{3,2,0,1:T(8,128)(2,1)}, bf16[1,32,256,1024]{3,2,0,1:T(8,128)(2,1)}) fusion(f32[32,256]{1,0:T(8,128)S(1)} %get-tuple-element.29, f32[1024]{0:T(1024)S(1)} %bitcast.90, f32[1024]{0:T(1024)S(1)} %bitcast.86, bf16[2,32,256,1024]{3,2,0,1:T(8,128)(2,1)} %bitcast.71, f32[32,256]{1,0:T(8,128)S(1)} %get-tuple-element.28, ...), kind=kLoop, calls=%fused_computation.9 | loop fusion | flops 83886080 | bytes 67190784 | tf_op jit(solution)/shard_map/convert_element_type | solution.py:32
  871.8 0.0 all-to-all-done.2
  871.8 13.6 %select_reduce_fusion.1 = f32[512]{0:T(512)S(1)} fusion(bf16[512,1024]{1,0:T(8,128)(2,1)S(1)} %bitcast.77, bf16[8192,1024]{1,0:T(8,128)(2,1)} %bitcast.75, s32[8192]{0:T(1024)S(1)} %bitcast.92, s32[512]{0:T(512)S(1)} %bitcast.96, pred[8192]{0:T(1024)(128)(4,1)S(1)} %iota_compare_fusion.2, pred[512]{0:T(512)(128)(4,1)S(1)} %bitcast.99), kind=kOutput, calls=%fused_computation.15 | convolution fusion | flops 8610906112 | bytes 17871360 | tf_op jit(solution)/shard_map/dot_general | solution.py:45
  885.4 0.0 copy-start.1
  885.4 13.7 %select_reduce_fusion = f32[512]{0:T(512)S(1)} fusion(bf16[512,1024]{1,0:T(8,128)(2,1)S(1)} %bitcast.78, bf16[8192,1024]{1,0:T(8,128)(2,1)} %bitcast.74, s32[8192]{0:T(1024)S(1)} %bitcast.91, s32[512]{0:T(512)S(1)} %bitcast.97, pred[8192]{0:T(1024)(128)(4,1)S(1)} %iota_compare_fusion.1, pred[512]{0:T(512)(128)(4,1)S(1)} %bitcast.98), kind=kOutput, calls=%fused_computation.14 | convolution fusion | flops 8610906112 | bytes 17871360 | tf_op jit(solution)/shard_map/dot_general | solution.py:45
  899.1 0.6 maximum_maximum_fusion
  899.7 4.8 all-to-all-start.3
  904.5 5.1 all-to-all-done.3
  909.6 1.9 gather_fusion.1
  911.6 0.6 and_select_fusion.1
  (23 shorter events, 0.2 us)
Async XLA Ops:
  0.0 383.4 %copy-start = (s32[256]{0:T(256)S(1)}, s32[256]{0:T(256)}, u32[]{:S(2)}) copy-start(s32[256]{0:T(256)} %param.12) | copy-start | bytes 3076
  0.0 2.9 collective-permute-start
  6.5 48.2 %collective-permute-start.1 = (bf16[2,2,256,1024]{3,2,1,0:T(8,128)(2,1)}, bf16[2,2,256,1024]{3,2,1,0:T(8,128)(2,1)}, u32[]{:S(2)}, u32[]{:S(2)}) collective-permute-start(bf16[2,2,256,1024]{3,2,1,0:T(8,128)(2,1)} %get-tuple-element.15), channel_id=1, source_target_pairs={{0,2},{1,3},{2,0},{3,1},{4,6},{5,7},{6,4},{7,5},{8,10},{9,11},{10,... | collective-permute-start | bytes 6291464 | tf_op jit(solution)/shard_map/ppermute | solution.py:20
  59.9 94.1 %collective-permute-start.2 = (bf16[4,2,256,1024]{3,2,1,0:T(8,128)(2,1)}, bf16[4,2,256,1024]{3,2,1,0:T(8,128)(2,1)}, u32[]{:S(2)}, u32[]{:S(2)}) collective-permute-start(bf16[4,2,256,1024]{3,2,1,0:T(8,128)(2,1)} %bitcast.20), channel_id=1, source_target_pairs={{0,4},{1,5},{2,6},{3,7},{4,0},{5,1},{6,2},{7,3},{8,12},{9,13},{10,... | collective-permute-start | bytes 12582920 | tf_op jit(solution)/shard_map/ppermute | solution.py:20
  175.0 181.4 %collective-permute-start.3 = (bf16[8,2,256,1024]{3,2,1,0:T(8,128)(2,1)}, bf16[8,2,256,1024]{3,2,1,0:T(8,128)(2,1)}, u32[]{:S(2)}, u32[]{:S(2)}) collective-permute-start(bf16[8,2,256,1024]{3,2,1,0:T(8,128)(2,1)} %bitcast.72), channel_id=1, source_target_pairs={{0,8},{1,9},{2,10},{3,11},{4,12},{5,13},{6,14},{7,15},{8,0},{9,1},... | collective-permute-start | bytes 25165832 | tf_op jit(solution)/shard_map/ppermute | solution.py:20
  364.4 13.6 %copy-start.7 = (s32[256]{0:T(256)S(1)}, s32[256]{0:T(256)}, u32[]{:S(2)}) copy-start(s32[256]{0:T(256)} %param.11) | copy-start | bytes 3076
  364.4 27.8 %copy-start.2 = (bf16[256,1024]{1,0:T(8,128)(2,1)S(1)}, bf16[256,1024]{1,0:T(8,128)(2,1)}, u32[]{:S(2)}) copy-start(bf16[256,1024]{1,0:T(8,128)(2,1)} %param.10) | copy-start | bytes 1572868
  364.4 30.2 %copy-start.5 = (s32[2,256]{1,0:T(2,128)S(1)}, s32[2,256]{1,0:T(2,128)}, u32[]{:S(2)}) copy-start(s32[2,256]{1,0:T(2,128)} %param.17) | copy-start | bytes 6148
  364.4 390.1 %copy-start.6 = (s32[2]{0:T(128)S(1)}, s32[2]{0:T(128)}, u32[]{:S(2)}) copy-start(s32[2]{0:T(128)} %param.16) | copy-start | bytes 28
  364.5 391.4 %copy-start.3 = (f32[2,1024]{1,0:T(2,128)S(1)}, f32[2,1024]{1,0:T(2,128)}, u32[]{:S(2)}) copy-start(f32[2,1024]{1,0:T(2,128)} %param.14) | copy-start | bytes 24580
  364.5 391.4 %copy-start.4 = (f32[2,1024]{1,0:T(2,128)S(1)}, f32[2,1024]{1,0:T(2,128)}, u32[]{:S(2)}) copy-start(f32[2,1024]{1,0:T(2,128)} %param.15) | copy-start | bytes 24580
  375.0 387.2 %collective-permute-start.4 = (bf16[16,2,256,1024]{3,2,1,0:T(8,128)(2,1)}, bf16[16,2,256,1024]{3,2,1,0:T(8,128)(2,1)}, u32[]{:S(2)}, u32[]{:S(2)}) collective-permute-start(bf16[16,2,256,1024]{3,2,1,0:T(8,128)(2,1)} %bitcast.26), channel_id=1, source_target_pairs={{0,16},{1,17},{2,18},{3,19},{4,20},{5,21},{6,22},{7,23},{8,24},{9,... | collective-permute-start | bytes 50331656 | tf_op jit(solution)/shard_map/ppermute | solution.py:20
  387.7 370.0 %all-to-all-start = ((s32[4,1,128]{2,1,0:T(1,128)}), s32[4,1,128]{2,1,0:T(1,128)S(1)}, u32[]{:S(2)}, u32[]{:S(2)}) async-start(s32[4,1,128]{2,1,0:T(1,128)} %bitcast.3), calls=%async_computation | async-start | bytes 4096 | tf_op jit(solution)/shard_map/all_to_all | solution.py:78
  757.7 80.8 %all-to-all-start.1 = ((s32[4,1,128]{2,1,0:T(1,128)}), s32[4,1,128]{2,1,0:T(1,128)S(1)}, u32[]{:S(2)}, u32[]{:S(2)}) async-start(s32[4,1,128]{2,1,0:T(1,128)} %bitcast.6), calls=%async_computation.1 | async-start | bytes 4096 | tf_op jit(solution)/shard_map/all_to_all | solution.py:79
  838.5 33.2 %all-to-all-start.2 = ((bf16[4,128,1024]{2,1,0:T(8,128)(2,1)}), bf16[4,128,1024]{2,1,0:T(8,128)(2,1)S(1)}, u32[]{:S(2)}, u32[]{:S(2)}) async-start(bf16[4,128,1024]{2,1,0:T(8,128)(2,1)} %broadcast_select_fusion), calls=%async_computation.2 | async-start | bytes 2097152 | tf_op jit(solution)/shard_map/all_to_all | solution.py:77
  885.4 26.7 %copy-start.1 = (s32[256]{0:T(256)S(1)}, s32[256]{0:T(256)}, u32[]{:S(2)}) copy-start(s32[256]{0:T(256)} %param.12) | copy-start | bytes 3076
  899.7 9.9 %all-to-all-start.3 = ((f32[4,1,128]{2,1,0:T(1,128)}), f32[4,1,128]{2,1,0:T(1,128)S(1)}, u32[]{:S(2)}, u32[]{:S(2)}) async-start(f32[4,1,128]{2,1,0:T(1,128)} %bitcast.39), calls=%async_computation.3 | async-start | bytes 4096 | tf_op jit(solution)/shard_map/all_to_all | solution.py:101
